TPU v7x, 32 devices: a whole 2x2x4 slice. The times are simulated.
32 devices in a mesh: ctx: 8 (over z, x), tp: 4 (over y, core).
Axes of the slice: x: 2, y: 2, z: 4, core: 2. Of those that a mesh axis runs over, the one named last changes fastest.
Arguments:
- projections: bfloat16 [2048, 3, 8192], P('ctx', None, 'tp'), may hold values from -6 to 6
- short_filter: float32 [3, 3, 8192], P(None, None, 'tp'), may hold values from -3 to 3
- decay_rates: float32 [16, 8192], P(None, 'tp'), may hold values from 1.4648437e-05 to 1
- residues: float32 [16, 8192], P(None, 'tp'), may hold values from -2.4 to 2.4
- out_weight: bfloat16 [8192, 4096], P('tp'), may hold values from -0.0625 to 0.0625
Outputs:
- projected: bfloat16 [2048, 4096], P(('ctx', 'tp'))
All inputs are finite; a program needn't handle non-finite values.
Results may differ from a plain program's by a relative error of at most 0.005.
Values may be sent and summed in bfloat16 or wider, within the bound.
A program may use at most 320 MiB of HBM per device.

v0:
```python
import jax
import jax.numpy as jnp
from jax import lax
from jax.sharding import PartitionSpec as P

STRETCH = 64


def shifted_2(block, axis, distance):
    devices = range(lax.axis_size(axis))
    route = [(i - distance, i) for i in devices if i - distance in devices]
    return lax.ppermute(block, axis, route)


def carried_in(part, axis, combine, identity):
    place = lax.axis_index(axis)
    gathered = jax.tree.map(lambda a: lax.all_gather(a, axis), part)
    state = jax.tree.map(lambda a, e: jnp.zeros_like(a) + jnp.asarray(e, a.dtype), part, identity)

    def one(step, state):
        return combine(
            state, jax.tree.map(lambda a: lax.dynamic_index_in_dim(a, step, 0, False), gathered)
        )

    return lax.fori_loop(0, place, one, state)


def make_tables(rates, weights_in, block_len):
    scaled = weights_in * jnp.sqrt(2.0 * rates)
    offsets = jnp.arange(block_len).astype(jnp.float32)
    hvalues = jnp.sum(scaled[None] * jnp.exp(-rates[None] * offsets[:, None, None]), axis=1)
    spread = jnp.arange(block_len)[:, None] - jnp.arange(block_len)[None, :]
    toeplitz = jnp.where(
        (spread >= 0)[:, :, None], hvalues[jnp.clip(spread, 0, block_len - 1)], 0.0
    )
    ending = jnp.exp(-rates[None] * (block_len - 1.0 - offsets)[:, None, None])
    entering = scaled[None] * jnp.exp(-rates[None] * (offsets + 1.0)[:, None, None])
    return (toeplitz, ending, entering)


def combine(earlier, later):
    return (earlier[0] * later[0], earlier[1] * later[0] + later[1])


def local_parts(product, rates, weights_in):
    tok_rows, channels = product.shape
    blocks_count = tok_rows // STRETCH
    toeplitz, ending, entering = make_tables(rates, weights_in, STRETCH)
    pieces = product.reshape(blocks_count, STRETCH, channels)
    hp = lax.Precision.HIGHEST
    inner = jnp.einsum("tsc,ksc->ktc", toeplitz, pieces, precision=hp)
    ends = jnp.einsum("snc,ksc->knc", ending, pieces, precision=hp)
    decays = jnp.broadcast_to(jnp.exp(-rates * STRETCH)[None], ends.shape)
    _, running = lax.associative_scan(combine, (decays, ends), axis=0)
    shifted = jnp.concatenate([jnp.zeros_like(running[:1]), running[:-1]], axis=0)
    return (inner, shifted, running[-1], entering)


def finish(inner, shifted, incoming, rates, entering):
    blocks_count, block_len, channels = inner.shape
    starts = (jnp.arange(blocks_count) * block_len).astype(jnp.float32)
    powers = jnp.exp(-rates[None] * starts[:, None, None])
    states_in = powers * incoming[None] + shifted
    outer = jnp.einsum("tnc,knc->ktc", entering, states_in, precision=lax.Precision.HIGHEST)
    return (inner + outer).reshape(blocks_count * block_len, channels)


def per_device(projections, short_filter, decay_rates, residues, out_weight):
    tok_rows = projections.shape[0]
    previous = shifted_2(projections[tok_rows - 2 :], "ctx", 1)
    extended = jnp.concatenate([previous, projections], axis=0).astype(jnp.float32)
    featured = (
        short_filter[0] * extended[2:]
        + short_filter[1] * extended[1:-1]
        + short_filter[2] * extended[:-2]
    )
    product = featured[:, 1, :] * featured[:, 2, :]
    inner, shifted, total, entering = local_parts(product, decay_rates, residues)
    span_decay = jnp.exp(-decay_rates * tok_rows)
    _, incoming = carried_in(
        (span_decay, total), "ctx", combine, (jnp.ones_like(total), jnp.zeros_like(total))
    )
    convolved = finish(inner, shifted, incoming, decay_rates, entering)
    gated = (featured[:, 0, :] * convolved).astype(jnp.bfloat16)
    summed = lax.psum_scatter(
        jnp.dot(gated, out_weight, preferred_element_type=jnp.float32),
        "tp",
        scatter_dimension=0,
        tiled=True,
    )
    return summed.astype(jnp.bfloat16)


def solution(mesh):
    placed = (
        P("ctx", None, "tp"),
        P(None, None, "tp"),
        P(None, "tp"),
        P(None, "tp"),
        P("tp", None),
    )
    return jax.shard_map(
        per_device, mesh=mesh, in_specs=placed, out_specs=P(("ctx", "tp"), None), check_vma=False
    )
```

profile of v0, /device:TPU:0, one launch (start us, length us, event | category | flops | bytes accessed | tf_op | source)
XLA Modules:
  0.0 371.5 jit_solution(5330285659145319484)
XLA Ops:
  6.5 0.0 all-gather.6.cloned.1.call-start
  6.5 0.9 slice.72
  7.5 5.4 %collective-permute-start = (bf16[2,3,2048]{2,0,1:T(2,128)(2,1)S(1)}, bf16[2,3,2048]{2,0,1:T(2,128)(2,1)}, u32[]{:S(2)}, u32[]{:S(2)}) collective-permute-start(bf16[2,3,2048]{2,0,1:T(2,128)(2,1)S(1)} %slice.72), channel_id=1, source_target_pairs={{0,4},{4,8},{8,12},{12,16},{16,20},{20,24},{24,28},{1,5},{5,9},{9,... | collective-permute-start | bytes 73736 | tf_op jit(solution)/shard_map/ppermute | solution.py:12
  12.9 1.7 multiply_exponential_fusion.1
  14.6 0.0 all-gather.6.cloned.1.call-update
  14.6 0.0 all-gather.4.cloned.1.call-start
  14.7 0.6 iota_convert_fusion
  15.3 0.5 broadcast_subtract_fusion
  15.8 0.5 multiply_convert_fusion
  16.3 0.8 slice_bitcast_fusion.3
  17.2 0.3 copy.64
  17.5 0.0 copy-start.5
  17.5 0.3 copy.63
  17.8 0.1 reshape.70
  17.9 12.4 %multiply_reduce_fusion = f32[64,2048]{0,1:T(8,128)S(1)} fusion(f32[64]{0:T(128)} %iota_convert_fusion, f32[16,2048]{0,1:T(8,128)S(1)} %copy.64, f32[16,2048]{0,1:T(8,128)S(1)} %copy.63), kind=kLoop, calls=%fused_computation.14 | loop fusion | flops 6160384 | bytes 786688 | tf_op jit(solution)/shard_map/reduce_sum | solution.py:31
  30.3 0.6 broadcast_add_fusion
  30.9 0.0 copy-done.5
  30.9 0.3 copy.65
  31.2 24.0 %gather_fusion = f32[4096,2048]{1,0:T(8,128)} fusion(f32[64,2048]{1,0:T(8,128)S(1)} %copy.65, s32[4096]{0:T(1024)S(1)} %broadcast_clamp_fusion), kind=kCustom, calls=%fused_computation | custom fusion | bytes 67125248 | tf_op jit(solution)/shard_map/gather | solution.py:34
  55.2 59.0 %copy.66 = f32[64,64,2048]{1,0,2:T(8,128)} copy(f32[64,64,2048]{2,1,0:T(8,128)} %bitcast.44) | data formatting | bytes 67108864 | tf_op jit(solution)/shard_map/gather | solution.py:34
  114.2 0.0 collective-permute-done
  114.2 1.7 maximum_convert_fusion
  115.9 1.9 fusion.16
  117.8 2.7 copy-done
  120.5 0.2 slice_multiply_fusion.3
  120.8 3.2 copy.67
  124.0 30.6 %fusion.8 = f32[2048,4,16]{2,1,0:T(4,128)} fusion(f32[4,64,2048]{1,0,2:T(4,128)} %copy.67, f32[64]{0:T(128)S(1)} %copy-done.10, f32[16,2048]{0,1:T(8,128)S(1)} %copy-done.6), kind=kOutput, calls=%fused_computation.11 | convolution fusion | flops 102760448 | bytes 2752768 | tf_op jit(solution)/shard_map/snc,ksc->knc/dot_general | solution.py:52
  154.6 3.4 copy.69
  158.2 0.1 pad.24
  158.3 0.1 pad.16
  158.4 0.1 pad.42
  158.5 0.7 slice_add_fusion.1
  159.2 0.0 all-gather.4.cloned.1.call-update
  159.2 0.0 copy-start.4
  159.2 0.0 copy-start.8
  159.2 0.0 reduce-scatter.2.cloned.1.call-start
  159.3 109.4 %fusion = f32[2048,4,64]{2,1,0:T(4,128)} fusion(f32[4,64,2048]{1,0,2:T(4,128)} %copy.67, f32[64,64,2048]{1,0,2:T(8,128)} %copy.66, pred[64,64]{1,0:T(8,128)(4,1)S(1)} %subtract_compare_fusion), kind=kOutput, calls=%fused_computation.3 | convolution fusion | flops 411041792 | bytes 37752832 | tf_op jit(solution)/shard_map/tsc,ksc->ktc/dot_general | solution.py:51
  268.7 0.0 all-gather.4.cloned.1.call-done
  268.7 0.2 pad_add_fusion
  268.9 3.3 copy.70
  272.2 0.0 copy-done.9
  272.2 24.5 %add_bitcast_fusion = f32[4,64,2048]{1,0,2:T(4,128)} fusion(f32[2048,4,64]{2,1,0:T(4,128)} %fusion, f32[4,16,2048]{1,0,2:T(4,128)} %copy.70, f32[64]{0:T(128)S(1)} %copy-done.9, f32[16,2048]{0,1:T(8,128)S(1)} %copy-done.6, f32[16,2048]{0,1:T(8,128)} %copy-done.7), kind=kOutput, calls=%fused_computation.25 | convolution fusion | flops 105381888 | bytes 4980992 | tf_op jit(solution)/shard_map/tnc,knc->ktc/dot_general | solution.py:64
  296.7 3.5 copy.71
  300.2 1.8 fusion.21
  302.0 10.1 %fusion.28 = f32[256,4096]{1,0:T(8,128)} fusion(bf16[256,2048]{1,0:T(8,128)(2,1)S(1)} %fusion.21, bf16[2048,4096]{1,0:T(8,128)(2,1)} %param.11), kind=kOutput, calls=%fused_computation.60 | convolution fusion | flops 4294967296 | bytes 22020096 | tf_op jit(solution)/shard_map/dot_general | solution.py:86
  312.1 0.0 reduce-scatter.2.cloned.1.call-update
  312.2 50.7 %reduce-scatter.2.cloned.1.call-done = f32[64,4096]{1,0:T(8,128)} async-done(((f32[256,4096]{1,0:T(8,128)}), f32[64,4096]{1,0:T(8,128)}) %reduce-scatter.2.cloned.1.call-update) | async-done | bytes 1048592 | tf_op jit(solution)/shard_map/reduce_scatter | solution.py:85
  362.9 2.1 convert_element_type.37
  (28 shorter events, 0.3 us)
Async XLA Ops:
  6.5 262.1 %all-gather.6.cloned.1.call-start = ((), (), s32[]{:S(2)}) async-start(), calls=%async_computation.3 | async-start | bytes 1179648 | tf_op jit(solution)/shard_map/all_gather | solution.py:17
  7.5 106.8 %collective-permute-start = (bf16[2,3,2048]{2,0,1:T(2,128)(2,1)S(1)}, bf16[2,3,2048]{2,0,1:T(2,128)(2,1)}, u32[]{:S(2)}, u32[]{:S(2)}) collective-permute-start(bf16[2,3,2048]{2,0,1:T(2,128)(2,1)S(1)} %slice.72), channel_id=1, source_target_pairs={{0,4},{4,8},{8,12},{12,16},{16,20},{20,24},{24,28},{1,5},{5,9},{9,... | collective-permute-start | bytes 73736 | tf_op jit(solution)/shard_map/ppermute | solution.py:12
  14.6 16.3 %copy-start.3 = (f32[16,2048]{1,0:T(8,128)}, f32[16,2048]{1,0:T(8,128)S(1)}, u32[]{:S(2)}) copy-start(f32[16,2048]{1,0:T(8,128)S(1)} %get-tuple-element.76) | copy-start | bytes 393220
  14.6 254.0 %all-gather.4.cloned.1.call-start = ((), (), s32[]{:S(2)}) async-start(), calls=%async_computation.1 | async-start | bytes 1179648 | tf_op jit(solution)/shard_map/all_gather | solution.py:17
  17.5 13.4 %copy-start.5 = (f32[16,2048]{0,1:T(8,128)}, f32[16,2048]{0,1:T(8,128)S(1)}, u32[]{:S(2)}) copy-start(f32[16,2048]{0,1:T(8,128)S(1)} %copy.64) | copy-start | bytes 393220
  17.8 37.4 %copy-start.7 = (f32[16,2048]{0,1:T(8,128)}, f32[16,2048]{0,1:T(8,128)S(1)}, u32[]{:S(2)}) copy-start(f32[16,2048]{0,1:T(8,128)S(1)} %copy.63) | copy-start | bytes 393220
  55.2 59.0 %copy-start.1 = (bf16[256,3,2048]{2,0,1:T(8,128)(2,1)S(1)}, bf16[256,3,2048]{2,0,1:T(8,128)(2,1)}, u32[]{:S(2)}) copy-start(bf16[256,3,2048]{2,0,1:T(8,128)(2,1)} %param.7) | copy-start | bytes 9437188
  117.8 2.7 copy-start
  120.5 3.5 copy-start.6
  120.5 3.5 copy-start.10
  124.0 34.1 %copy-start.2 = (f32[16,2048]{1,0:T(8,128)S(1)}, f32[16,2048]{1,0:T(8,128)}, u32[]{:S(2)}) copy-start(f32[16,2048]{1,0:T(8,128)} %param.9) | copy-start | bytes 393220
  159.2 109.5 %copy-start.4 = (f32[16,2048]{1,0:T(8,128)S(1)}, f32[16,2048]{1,0:T(8,128)}, u32[]{:S(2)}) copy-start(f32[16,2048]{1,0:T(8,128)} %copy-done.3) | copy-start | bytes 393220
  159.2 109.5 %copy-start.8 = (f32[4]{0:T(128)S(1)}, f32[4]{0:T(128)}, u32[]{:S(2)}) copy-start(f32[4]{0:T(128)} %multiply_convert_fusion) | copy-start | bytes 52
  159.2 203.6 %reduce-scatter.2.cloned.1.call-start = ((), (), s32[]{:S(2)}) async-start(), calls=%async_computation.2 | async-start | bytes 5242880 | tf_op jit(solution)/shard_map/reduce_scatter | solution.py:85
  268.7 3.6 copy-start.9
Sparse Core Ops, SparseCore 0:
  14.8 39.8 all-gather.5
  159.3 39.8 all-gather.3
  312.3 50.5 reduce-scatter.1
where the time goes:
time: 373 us; the launch traced here: 371 us
  matrix products  175 us (47%)
  local copies, waits for them, and re-layouts  102 us (27%)
  waiting for transfers between devices  50.8 us (14%)
  other arithmetic  25.1 us (7%)
  between operations  13.3 us (4%)
  starting transfers between devices  5.53 us (1%)
    dot_general x1, matrix products, local_parts(): inner = jnp.einsum('tsc,ksc->ktc', toeplitz, pieces, precision=hp)  109 us
    gather x2, local copies, waits for them, and re-layouts, make_tables(): hvalues[jnp.clip(spread, 0, block_len - 1)]  83 us
    reduce_scatter x1, waiting for transfers between devices, per_device(): lax.psum_scatter(jnp.dot(gated, out_weight, preferred_element_type=jnp.fl...  50.7 us
    dot_general x1, matrix products, local_parts(): ends = jnp.einsum('snc,ksc->knc', ending, pieces, precision=hp)  30.6 us
    dot_general x1, matrix products, finish(): jnp.einsum('tnc,knc->ktc', entering, states_in, precision=lax.Precision.H...  24.5 us
    reduce_sum x1, other arithmetic, make_tables(): jnp.sum(scaled[None] * jnp.exp(-rates[None] * offsets[:, None, None]), ax...  12.4 us
    dot_general x1, matrix products, per_device(): jnp.dot(gated, out_weight, preferred_element_type=jnp.float32)  10.1 us
  transfers between devices with their start and end apart: 4, of which 1 were waited for; matrix products, arithmetic and copies ran while one was open for 68% of the time, Pallas kernels for 0%

commit v1 on v0

v1 whole, which is shorter than its diff:
```python
import functools

import jax
import jax.numpy as jnp
from jax import lax
from jax.experimental import pallas as pl
from jax.experimental.pallas import tpu as pltpu
from jax.sharding import PartitionSpec as P

LANES = 128
CHUNKS = 8
PAD = 8
GROUPS = 4
WIDTH = 512
UNROLL = 8
MESH = pl.DeviceIdType.MESH
F32 = jnp.float32
BF16 = jnp.bfloat16


def kernel(
    n_ctx, x_hbm, taps_ref, rates_ref, res_ref, w_hbm, out_ref,
    xb, xs, yl, qf, gb, wv, pt, excl, halo_out, halo_in, st_out, st_in,
    decay_all, carry, keep, pair_out, pair_in, far_out, far_in,
    x_sem, w_sem, halo_sem, st_send, st_recv, pair_send, pair_recv, far_send, far_recv,
):
    me = lax.axis_index("ctx")
    tp = lax.axis_index("tp")
    chip, core = tp // 2, tp % 2
    sibling = chip * 2 + (1 - core)
    opposite = (1 - chip) * 2 + core
    toks, channels = xb.shape[1], xb.shape[2]
    step = toks // CHUNKS
    tiles = channels // LANES
    per_group = tiles // GROUPS
    gwidth = channels // GROUPS
    n_out = w_hbm.shape[1] // WIDTH
    share = toks // 4

    x_copy = pltpu.make_async_copy(x_hbm, xb, x_sem)
    x_copy.start()
    w_copy = pltpu.make_async_copy(w_hbm, wv, w_sem)

    barrier = pltpu.get_barrier_semaphore()

    @pl.loop(1, n_ctx)
    def _(k):
        pl.semaphore_signal(
            barrier, inc=1, device_id=(lax.rem(me + k, n_ctx), tp), device_id_type=MESH
        )

    for other in (sibling, opposite):
        pl.semaphore_signal(barrier, inc=1, device_id=(me, other), device_id_type=MESH)

    x_copy.wait()
    w_copy.start()
    for j in range(3):
        tail = xb[j, toks - 16 :, :].astype(F32)
        halo_out[2 * j : 2 * j + 2, :] = tail[14:16]
    halo_out[6:8, :] = jnp.zeros((2, channels), F32)

    pl.semaphore_wait(barrier, n_ctx + 1)

    halo_copy = pltpu.make_async_remote_copy(
        src_ref=halo_out, dst_ref=halo_in, send_sem=halo_sem.at[0], recv_sem=halo_sem.at[1],
        device_id=(lax.rem(me + 1, n_ctx), tp), device_id_type=MESH,
    )

    @pl.when(me < n_ctx - 1)
    def _():
        halo_copy.start()

    @pl.loop(0, tiles)
    def _(c):
        lane = pl.ds(pl.multiple_of(c * LANES, LANES), LANES)
        for j in range(3):
            xs[j, c, PAD:, :] = xb[j, :, lane].astype(F32)

    @pl.when(me == 0)
    def _():
        halo_in[...] = jnp.zeros_like(halo_in)

    @pl.when(me > 0)
    def _():
        halo_copy.wait_recv()

    place = lax.broadcasted_iota(jnp.int32, (1, CHUNKS, LANES), 1)

    def spread(rows):
        return jnp.broadcast_to(rows[:, None, :], (rows.shape[0], CHUNKS, LANES))

    def local_tile(c):
        lane = pl.ds(pl.multiple_of(c * LANES, LANES), LANES)
        rates = rates_ref[:, lane]
        decay = spread(jnp.exp(-rates))
        weight = spread(res_ref[:, lane] * jnp.sqrt(2.0 * rates))
        taps = [[spread(taps_ref[i, j : j + 1, lane])[0] for j in range(3)] for i in range(3)]
        for j in range(3):
            xs[j, c, PAD - 2 : PAD, :] = halo_in[2 * j : 2 * j + 2, lane]

        def at(j, row):
            return xs[j, c, pl.ds(row, CHUNKS, stride=step), :]

        def some(outer, held):
            state, before = held
            before = list(before)
            for k in range(UNROLL):
                i = outer * UNROLL + k
                feats = []
                for j in range(3):
                    now = at(j, PAD + i)
                    one, two = before[2 * j], before[2 * j + 1]
                    feats.append(taps[0][j] * now + taps[1][j] * one + taps[2][j] * two)
                    before[2 * j], before[2 * j + 1] = now, one
                product = feats[1] * feats[2]
                state = decay * state + product[None]
                rows = pl.ds(i, CHUNKS, stride=step)
                yl[c, rows, :] = jnp.sum(weight * state, axis=0)
                qf[c, rows, :] = feats[0]
            return state, tuple(before)

        before = []
        for j in range(3):
            before += [at(j, PAD - 1), at(j, PAD - 2)]
        modes = rates.shape[0]
        zero = jnp.zeros((modes, CHUNKS, LANES), F32)
        state, _ = lax.fori_loop(0, step // UNROLL, some, (zero, tuple(before)))
        for reach in (1, 2, 4):
            fade = spread(jnp.exp(-rates * float(step * reach)))
            moved = pltpu.roll(state, reach, 1)
            state = state + jnp.where(place >= reach, fade * moved, 0.0)
        excl[c] = jnp.where(place >= 1, pltpu.roll(state, 1, 1), 0.0)
        st_out[:, lane] = state[:, CHUNKS - 1, :].astype(BF16)
        decay_all[:, lane] = jnp.exp(-rates * float(toks))

    def state_copy(g, src, dst):
        cols = pl.ds(g * gwidth, gwidth)
        return pltpu.make_async_remote_copy(
            src_ref=st_out.at[:, cols], dst_ref=st_in.at[src, :, cols],
            send_sem=st_send.at[dst, g], recv_sem=st_recv.at[src, g],
            device_id=(dst, tp), device_id_type=MESH,
        )

    for g in range(GROUPS):
        @pl.loop(g * per_group, (g + 1) * per_group)
        def _(c):
            local_tile(c)

        @pl.loop(me + 1, n_ctx)
        def _(dst):
            state_copy(g, me, dst).start()

    def carried_tile(c):
        lane = pl.ds(pl.multiple_of(c * LANES, LANES), LANES)
        rates = rates_ref[:, lane]
        decay = spread(jnp.exp(-rates))
        weight = res_ref[:, lane] * jnp.sqrt(2.0 * rates) * jnp.exp(-rates)
        starts = (place * step).astype(F32)
        into = excl[c] + jnp.exp(-spread(rates) * starts) * spread(carry[:, lane])
        state = spread(weight) * into

        def some(outer, state):
            for k in range(UNROLL):
                rows = pl.ds(outer * UNROLL + k, CHUNKS, stride=step)
                yl[c, rows, :] = qf[c, rows, :] * (yl[c, rows, :] + jnp.sum(state, axis=0))
                state = decay * state
            return state

        lax.fori_loop(0, step // UNROLL, some, state)
        gb[:, lane] = yl[c].astype(BF16)

    for g in range(GROUPS):
        cols = pl.ds(g * gwidth, gwidth)
        carry[:, cols] = jnp.zeros((carry.shape[0], gwidth), F32)

        @pl.loop(0, me)
        def _(src):
            state_copy(g, src, me).wait_recv()
            carry[:, cols] = decay_all[:, cols] * carry[:, cols] + st_in[src, :, cols].astype(F32)

        @pl.loop(g * per_group, (g + 1) * per_group)
        def _(c):
            carried_tile(c)

    w_copy.wait()

    def pair_copy(n):
        return pltpu.make_async_remote_copy(
            src_ref=pair_out.at[n], dst_ref=pair_in.at[n],
            send_sem=pair_send.at[n], recv_sem=pair_recv.at[n],
            device_id=(me, sibling), device_id_type=MESH,
        )

    def far_copy(n):
        return pltpu.make_async_remote_copy(
            src_ref=far_out.at[n], dst_ref=far_in.at[n],
            send_sem=far_send.at[n], recv_sem=far_recv.at[n],
            device_id=(me, opposite), device_id_type=MESH,
        )

    def rows_of(which_chip, which_core):
        at = pl.multiple_of((which_chip * 2 + which_core) * share, share)
        return pl.ds(at, share)

    def forward(n):
        pair_copy(n).wait_recv()
        got = keep[n] + pair_in[n].astype(F32)
        far_out[n] = got[:share].astype(BF16)
        far_copy(n).start()
        keep[n, share:, :] = got[share:]

    @pl.loop(0, n_out)
    def _(n):
        cols = pl.ds(pl.multiple_of(n * WIDTH, WIDTH), WIDTH)
        pt[...] = jnp.dot(gb[...], wv[:, cols], preferred_element_type=F32)
        pair_out[n, :share, :] = pt[rows_of(1 - chip, 1 - core), :].astype(BF16)
        pair_out[n, share:, :] = pt[rows_of(chip, 1 - core), :].astype(BF16)
        pair_copy(n).start()
        keep[n, :share, :] = pt[rows_of(1 - chip, core), :]
        keep[n, share:, :] = pt[rows_of(chip, core), :]

        @pl.when(n > 0)
        def _():
            forward(n - 1)

    forward(n_out - 1)

    @pl.loop(0, n_out)
    def _(n):
        cols = pl.ds(pl.multiple_of(n * WIDTH, WIDTH), WIDTH)
        far_copy(n).wait_recv()
        out_ref[:, cols] = (keep[n, share:, :] + far_in[n].astype(F32)).astype(BF16)

    @pl.loop(0, n_out)
    def _(n):
        pair_copy(n).wait_send()
        far_copy(n).wait_send()

    for g in range(GROUPS):
        @pl.loop(me + 1, n_ctx)
        def _(dst):
            state_copy(g, me, dst).wait_send()

    @pl.when(me < n_ctx - 1)
    def _():
        halo_copy.wait_send()


def per_device(n_ctx, projections, short_filter, decay_rates, residues, out_weight):
    x = jnp.transpose(projections, (1, 0, 2))
    _, toks, channels = x.shape
    modes = decay_rates.shape[0]
    dout = out_weight.shape[1]
    tiles = channels // LANES
    n_out = dout // WIDTH
    share = toks // 4
    dma = pltpu.SemaphoreType.DMA
    vmem = pl.BlockSpec(memory_space=pltpu.VMEM)
    hbm = pl.BlockSpec(memory_space=pl.ANY)
    return pl.pallas_call(
        functools.partial(kernel, n_ctx),
        out_shape=jax.ShapeDtypeStruct((share, dout), BF16),
        in_specs=[hbm, vmem, vmem, vmem, hbm],
        out_specs=vmem,
        scratch_shapes=[
            pltpu.VMEM((3, toks, channels), BF16),
            pltpu.VMEM((3, tiles, PAD + toks, LANES), F32),
            pltpu.VMEM((tiles, toks, LANES), F32),
            pltpu.VMEM((tiles, toks, LANES), F32),
            pltpu.VMEM((toks, channels), BF16),
            pltpu.VMEM((channels, dout), BF16),
            pltpu.VMEM((toks, WIDTH), F32),
            pltpu.VMEM((tiles, modes, CHUNKS, LANES), F32),
            pltpu.VMEM((8, channels), F32),
            pltpu.VMEM((8, channels), F32),
            pltpu.VMEM((modes, channels), BF16),
            pltpu.VMEM((n_ctx, modes, channels), BF16),
            pltpu.VMEM((modes, channels), F32),
            pltpu.VMEM((modes, channels), F32),
            pltpu.VMEM((n_out, 2 * share, WIDTH), F32),
            pltpu.VMEM((n_out, 2 * share, WIDTH), BF16),
            pltpu.VMEM((n_out, 2 * share, WIDTH), BF16),
            pltpu.VMEM((n_out, share, WIDTH), BF16),
            pltpu.VMEM((n_out, share, WIDTH), BF16),
            dma, dma, dma((2,)),
            dma((n_ctx, GROUPS)), dma((n_ctx, GROUPS)),
            dma((n_out,)), dma((n_out,)), dma((n_out,)), dma((n_out,)),
        ],
        compiler_params=pltpu.CompilerParams(
            collective_id=0, has_side_effects=True, vmem_limit_bytes=58 * 2**20
        ),
    )(x, short_filter, decay_rates, residues, out_weight)


def solution(mesh):
    placed = (
        P("ctx", None, "tp"),
        P(None, None, "tp"),
        P(None, "tp"),
        P(None, "tp"),
        P("tp", None),
    )
    return jax.shard_map(
        functools.partial(per_device, mesh.shape["ctx"]),
        mesh=mesh, in_specs=placed, out_specs=P(("ctx", "tp"), None), check_vma=False,
    )
```

time: 373 us -> 45.8 us (0.12)
  matrix products: 175 us -> 0 us
  local copies, waits for them, and re-layouts: 102 us -> 1.87 us
  waiting for transfers between devices: 50.8 us -> 0 us
  Pallas kernels: 0 us -> 43.2 us
  other arithmetic: 25.1 us -> 0 us
  between operations: 13.3 us -> 0.01 us
  starting transfers between devices: 5.53 us -> 0 us
    dot_general x4 -> x0, matrix products: 175 us -> none  [the longest x1 109 us: local_parts(): inner = jnp.einsum('tsc,ksc->ktc', toeplitz, pieces, precision=hp)]
    gather x2 -> x0, local copies, waits for them, and re-layouts: 83 us -> none  [make_tables(): hvalues[jnp.clip(spread, 0, block_len - 1)]]
    reduce_scatter x1 -> x0, waiting for transfers between devices: 50.7 us -> none  [per_device(): lax.psum_scatter(jnp.dot(gated, out_weight, preferred_element_type=jnp.fl...]
    pallas_call x0 -> x1, Pallas kernels: none -> 43.2 us  [per_device(): pl.pallas_call(functools.partial(kernel, n_ctx), out_shape=jax.ShapeDtype...]
    reduce_sum x1 -> x0, other arithmetic: 12.4 us -> none  [make_tables(): jnp.sum(scaled[None] * jnp.exp(-rates[None] * offsets[:, None, None]), ax...]
    add x2 -> x0, local copies, waits for them, and re-layouts: 6.83 us -> none  [the longest x1 3.51 us: finish(): return (inner + outer).reshape(blocks_count * block_len, channels)]
    convert_element_type x5 -> x0, other arithmetic: 6.71 us -> none  [the longest x1 2.07 us: per_device(): return summed.astype(jnp.bfloat16)]
    ppermute x1 -> x0, starting transfers between devices: 5.45 us -> none  [shifted_2(): return lax.ppermute(block, axis, route)]
  transfers between devices with their start and end apart: 4 -> 0, of which waited for: 1 -> 0; matrix products, arithmetic and copies ran while one was open for 68% -> 0% of each run, Pallas kernels for 0% -> 0%
where the time goes in v1:
time: 45.8 us; the launch traced here: 45.1 us
  Pallas kernels  43.2 us (94%)
  local copies, waits for them, and re-layouts  1.87 us (4%)
    pallas_call x1, Pallas kernels, per_device(): pl.pallas_call(functools.partial(kernel, n_ctx), out_shape=jax.ShapeDtype...  43.2 us
    unnamed x1, local copies, waits for them, and re-layouts  1.87 us

profile of v1, /device:TPU:0, one launch (start us, length us, event | category | flops | bytes accessed | tf_op | source)
XLA Modules:
  0.0 45.1 jit_solution(12466692751276966309)
XLA Ops:
  0.0 43.2 %shard_map.55 = bf16[64,4096]{1,0:T(8,128)(2,1)} custom-call(bf16[3,256,2048]{2,1,0:T(8,128)(2,1)} %bitcast.1, f32[3,3,2048]{2,1,0:T(4,128)} %taps_ref.1, f32[16,2048]{1,0:T(8,128)} %rates_ref.1, f32[16,2048]{1,0:T(8,128)} %res_ref.1, bf16[2048,4096]{1,0:T(8,128)(2,1)} %w_hbm.1), custom_call_target="tpu_custom_call" | custom-call | tf_op jit(solution)/shard_map/pallas_call | solution.py:260
  43.2 1.9 %copy.7 = bf16[64,4096]{1,0:T(8,128)(2,1)} copy(bf16[64,4096]{1,0:T(8,128)(2,1)} %shard_map.55) | data formatting | bytes 1048576

commit v2 on v1

v2 whole, which is shorter than its diff:
```python
import functools

import jax
import jax.numpy as jnp
from jax import lax
from jax.experimental import pallas as pl
from jax.experimental.pallas import tpu as pltpu
from jax.sharding import PartitionSpec as P

LANES = 128
CHUNKS = 8
PAD = 8
GROUPS = 4
WIDTH = 512
UNROLL = 8
MESH = pl.DeviceIdType.MESH
F32 = jnp.float32
BF16 = jnp.bfloat16


def summed(terms):
    while terms.shape[0] % 2 == 0:
        middle = terms.shape[0] // 2
        terms = terms[:middle] + terms[middle:]
    return jnp.sum(terms, axis=0)


def kernel(
    n_ctx, x_hbm, taps_ref, rates_ref, res_ref, w_hbm, out_ref,
    xb, xs, pf, qf, yl, gs, ga, gb, wv, pt, excl, fades, halo_out, halo_in, st_out, twin_in, both_out, st_in,
    own_end, decay_all, carry, first, keep, kept, pair_out, pair_in, own_out, own_in, far_out, far_in,
    x_sem, w_sem, halo_sem, twin_send, twin_recv, st_send, st_recv,
    pair_send, pair_recv, own_send, own_recv, far_send, far_recv,
):
    me = lax.axis_index("ctx")
    tp = lax.axis_index("tp")
    pair, odd = me // 2, me % 2
    twin = pair * 2 + (1 - odd)
    chip, core = tp // 2, tp % 2
    sibling = chip * 2 + (1 - core)
    opposite = (1 - chip) * 2 + core
    toks, channels = xb.shape[1], xb.shape[2]
    half = toks // 2
    step = half // CHUNKS
    tiles = channels // LANES
    per_group = tiles // GROUPS
    gwidth = channels // GROUPS
    n_out = w_hbm.shape[1] // WIDTH
    share = toks // 4
    base_a = pl.multiple_of((1 - chip) * half, half)
    base_b = pl.multiple_of(chip * half, half)

    x_copy = pltpu.make_async_copy(x_hbm, xb, x_sem)
    x_copy.start()
    w_copy = pltpu.make_async_copy(w_hbm, wv, w_sem)

    barrier = pltpu.get_barrier_semaphore()

    @pl.loop(1, n_ctx)
    def _(k):
        pl.semaphore_signal(
            barrier, inc=1, device_id=(lax.rem(me + k, n_ctx), tp), device_id_type=MESH
        )

    for other in (sibling, opposite):
        pl.semaphore_signal(barrier, inc=1, device_id=(me, other), device_id_type=MESH)

    x_copy.wait()
    w_copy.start()
    for j in range(3):
        tail = xb[j, toks - 16 :, :].astype(F32)
        halo_out[2 * j : 2 * j + 2, :] = tail[14:16]
    halo_out[6:8, :] = jnp.zeros((2, channels), F32)

    pl.semaphore_wait(barrier, n_ctx + 1)

    halo_copy = pltpu.make_async_remote_copy(
        src_ref=halo_out, dst_ref=halo_in, send_sem=halo_sem.at[0], recv_sem=halo_sem.at[1],
        device_id=(lax.rem(me + 1, n_ctx), tp), device_id_type=MESH,
    )

    @pl.when(me < n_ctx - 1)
    def _():
        halo_copy.start()

    def features(c, lane, rows):
        feats = []
        for j in range(3):
            total = taps_ref[0, j : j + 1, lane] * xs[j, c, PAD : PAD + rows, :]
            for i in (1, 2):
                total += taps_ref[i, j : j + 1, lane] * xs[j, c, PAD - i : PAD - i + rows, :]
            feats.append(total)
        qf[c, :rows, :] = feats[0]
        pf[c, :rows, :] = feats[1] * feats[2]

    @pl.loop(0, tiles)
    def _(c):
        lane = pl.ds(pl.multiple_of(c * LANES, LANES), LANES)
        for j in range(3):
            xs[j, c, :PAD, :] = jnp.zeros((PAD, LANES), F32)
            xs[j, c, PAD:, :] = xb[j, :, lane].astype(F32)
        features(c, lane, toks)

    @pl.when(me == 0)
    def _():
        halo_in[...] = jnp.zeros_like(halo_in)

    @pl.when(me > 0)
    def _():
        halo_copy.wait_recv()

    place = lax.broadcasted_iota(jnp.int32, (1, CHUNKS, LANES), 1)

    def spread(rows):
        return jnp.broadcast_to(rows[:, None, :], (rows.shape[0], CHUNKS, LANES))

    def scanned(state, rates):
        for reach in (1, 2, 4):
            fade = spread(jnp.exp(-rates * float(step * reach)))
            moved = pltpu.roll(state, reach, 1)
            state = state + jnp.where(place >= reach, fade * moved, 0.0)
        return jnp.where(place >= 1, pltpu.roll(state, 1, 1), 0.0), state[:, CHUNKS - 1, :]

    def local_tile(c):
        lane = pl.ds(pl.multiple_of(c * LANES, LANES), LANES)
        rates = rates_ref[:, lane]
        decay = spread(jnp.exp(-rates))
        weight = spread(res_ref[:, lane] * jnp.sqrt(2.0 * rates))
        for j in range(3):
            xs[j, c, PAD - 2 : PAD, :] = halo_in[2 * j : 2 * j + 2, lane]
        features(c, lane, 8)
        zero = jnp.zeros((rates.shape[0], CHUNKS, LANES), F32)

        def ends(outer, state):
            for k in range(UNROLL):
                rows = pl.ds(base_b + outer * UNROLL + k, CHUNKS, stride=step)
                state = decay * state + pf[c, rows, :][None]
            return state

        before_b, total_b = scanned(lax.fori_loop(0, step // UNROLL, ends, zero), rates)
        excl[1, c] = before_b

        def both(outer, state):
            for k in range(UNROLL):
                rows = pl.ds(base_a + outer * UNROLL + k, CHUNKS, stride=step)
                state = decay * state + pf[c, rows, :][None]
                yl[c, pl.ds(outer * UNROLL + k, CHUNKS, stride=step), :] = summed(weight * state)
            return state

        before_a, total_a = scanned(lax.fori_loop(0, step // UNROLL, both, zero), rates)
        excl[0, c] = before_a
        fade = jnp.exp(-rates * float(half))
        early = jnp.where(chip == 0, total_b, total_a)
        late = jnp.where(chip == 0, total_a, total_b)
        first[:, lane] = early
        end = fade * early + late
        own_end[:, lane] = end
        st_out[:, lane] = end.astype(BF16)
        decay_all[:, lane] = jnp.exp(-rates * float(toks))

    def group(g):
        return pl.ds(g * gwidth, gwidth)

    def twin_copy(g):
        return pltpu.make_async_remote_copy(
            src_ref=st_out.at[:, group(g)], dst_ref=twin_in.at[:, group(g)],
            send_sem=twin_send.at[g], recv_sem=twin_recv.at[g],
            device_id=(twin, tp), device_id_type=MESH,
        )

    def state_copy(g, src, dst):
        return pltpu.make_async_remote_copy(
            src_ref=both_out.at[:, group(g)], dst_ref=st_in.at[src, :, group(g)],
            send_sem=st_send.at[dst, g], recv_sem=st_recv.at[src, g],
            device_id=(dst * 2 + odd, tp), device_id_type=MESH,
        )

    def send_both(g):
        cols = group(g)
        twin_copy(g).wait_recv()
        other = twin_in[:, cols].astype(F32)
        own = own_end[:, cols]
        fade = decay_all[:, cols]
        total = jnp.where(odd == 1, fade * other + own, fade * own + other)
        both_out[:, cols] = total.astype(BF16)

        @pl.loop(pair + 1, n_ctx // 2)
        def _(dst):
            state_copy(g, pair, dst).start()

    for g in range(GROUPS):
        @pl.loop(g * per_group, (g + 1) * per_group)
        def _(c):
            local_tile(c)

        twin_copy(g).start()
        if g > 0:
            send_both(g - 1)
    send_both(GROUPS - 1)

    def steady(c):
        lane = pl.ds(pl.multiple_of(c * LANES, LANES), LANES)
        rates = rates_ref[:, lane]
        weight = spread(res_ref[:, lane] * jnp.sqrt(2.0 * rates) * jnp.exp(-rates))
        starts = (place * step).astype(F32)
        fade = weight * jnp.exp(-spread(rates) * starts)
        base = weight * excl[0, c]
        fades[c] = fade
        excl[0, c] = base + jnp.where(chip == 0, fade * spread(first[:, lane]), 0.0)

    @pl.loop(0, tiles)
    def _(c):
        steady(c)

    def entering(c, lane, rates):
        starts = (place * step).astype(F32)
        into = carry[:, lane]
        late = jnp.exp(-rates * float(half)) * into + first[:, lane]
        into = jnp.where(chip == 1, late, into)
        return excl[1, c] + jnp.exp(-spread(rates) * starts) * spread(into)

    def carried_tile(c):
        lane = pl.ds(pl.multiple_of(c * LANES, LANES), LANES)
        rates = rates_ref[:, lane]
        decay = spread(jnp.exp(-rates))
        into = carry[:, lane]
        into = jnp.where(chip == 0, jnp.exp(-rates * float(half)) * into, into)
        state = excl[0, c] + fades[c] * spread(into)

        def some(outer, state):
            for k in range(UNROLL):
                i = outer * UNROLL + k
                local = pl.ds(i, CHUNKS, stride=step)
                gate = qf[c, pl.ds(base_a + i, CHUNKS, stride=step), :]
                gs[local, :] = gate * (yl[c, local, :] + summed(state))
                state = decay * state
            return state

        lax.fori_loop(0, step // UNROLL, some, state)
        ga[:, lane] = gs[...].astype(BF16)

    def own_tile(c):
        lane = pl.ds(pl.multiple_of(c * LANES, LANES), LANES)
        rates = rates_ref[:, lane]
        decay = spread(jnp.exp(-rates))
        weight = spread(res_ref[:, lane] * jnp.sqrt(2.0 * rates))
        state = entering(c, lane, rates)

        def some(outer, state):
            for k in range(UNROLL):
                i = outer * UNROLL + k
                rows = pl.ds(base_b + i, CHUNKS, stride=step)
                state = decay * state + pf[c, rows, :][None]
                gs[pl.ds(i, CHUNKS, stride=step), :] = qf[c, rows, :] * summed(weight * state)
            return state

        lax.fori_loop(0, step // UNROLL, some, state)
        gb[:, lane] = gs[...].astype(BF16)

    for g in range(GROUPS):
        cols = group(g)
        carry[:, cols] = jnp.zeros((carry.shape[0], gwidth), F32)

        @pl.loop(0, pair)
        def _(src):
            fade = decay_all[:, cols] * decay_all[:, cols]
            state_copy(g, src, pair).wait_recv()
            carry[:, cols] = fade * carry[:, cols] + st_in[src, :, cols].astype(F32)

        @pl.when(odd == 1)
        def _():
            carry[:, cols] = decay_all[:, cols] * carry[:, cols] + twin_in[:, cols].astype(F32)

        @pl.loop(g * per_group, (g + 1) * per_group)
        def _(c):
            carried_tile(c)

    w_copy.wait()

    def to_sibling(n, out, into, send, recv):
        return pltpu.make_async_remote_copy(
            src_ref=out.at[n], dst_ref=into.at[n], send_sem=send.at[n], recv_sem=recv.at[n],
            device_id=(me, sibling), device_id_type=MESH,
        )

    def pair_copy(n):
        return to_sibling(n, pair_out, pair_in, pair_send, pair_recv)

    def own_copy(n):
        return to_sibling(n, own_out, own_in, own_send, own_recv)

    def far_copy(n):
        return pltpu.make_async_remote_copy(
            src_ref=far_out.at[n], dst_ref=far_in.at[n],
            send_sem=far_send.at[n], recv_sem=far_recv.at[n],
            device_id=(me, opposite), device_id_type=MESH,
        )

    mine = pl.ds(pl.multiple_of(core * share, share), share)
    theirs = pl.ds(pl.multiple_of((1 - core) * share, share), share)

    def forward(n):
        pair_copy(n).wait_recv()
        far_out[n] = (keep[n] + pair_in[n].astype(F32)).astype(BF16)
        far_copy(n).start()

    def columns(n):
        return pl.ds(pl.multiple_of(n * WIDTH, WIDTH), WIDTH)

    @pl.loop(0, n_out)
    def _(n):
        pt[...] = jnp.dot(ga[...], wv[:, columns(n)], preferred_element_type=F32)
        pair_out[n] = pt[theirs, :].astype(BF16)
        pair_copy(n).start()
        keep[n] = pt[mine, :]

        @pl.when(n > 0)
        def _():
            forward(n - 1)

    forward(n_out - 1)

    @pl.loop(0, tiles)
    def _(c):
        own_tile(c)

    @pl.loop(0, n_out)
    def _(n):
        pt[...] = jnp.dot(gb[...], wv[:, columns(n)], preferred_element_type=F32)
        own_out[n] = pt[theirs, :].astype(BF16)
        own_copy(n).start()
        kept[n] = pt[mine, :]

    @pl.loop(0, n_out)
    def _(n):
        own_copy(n).wait_recv()
        far_copy(n).wait_recv()
        total = kept[n] + own_in[n].astype(F32) + far_in[n].astype(F32)
        out_ref[:, columns(n)] = total.astype(BF16)

    @pl.loop(0, n_out)
    def _(n):
        pair_copy(n).wait_send()
        own_copy(n).wait_send()
        far_copy(n).wait_send()

    for g in range(GROUPS):
        twin_copy(g).wait_send()

        @pl.loop(pair + 1, n_ctx // 2)
        def _(dst):
            state_copy(g, pair, dst).wait_send()

    @pl.when(me < n_ctx - 1)
    def _():
        halo_copy.wait_send()


def per_device(n_ctx, projections, short_filter, decay_rates, residues, out_weight):
    x = jnp.transpose(projections, (1, 0, 2))
    _, toks, channels = x.shape
    modes = decay_rates.shape[0]
    dout = out_weight.shape[1]
    tiles = channels // LANES
    n_out = dout // WIDTH
    share = toks // 4
    dma = pltpu.SemaphoreType.DMA
    vmem = pl.BlockSpec(memory_space=pltpu.VMEM)
    hbm = pl.BlockSpec(memory_space=pl.ANY)
    return pl.pallas_call(
        functools.partial(kernel, n_ctx),
        out_shape=jax.ShapeDtypeStruct((share, dout), BF16),
        in_specs=[hbm, vmem, vmem, vmem, hbm],
        out_specs=vmem,
        scratch_shapes=[
            pltpu.VMEM((3, toks, channels), BF16),
            pltpu.VMEM((3, tiles, PAD + toks, LANES), F32),
            pltpu.VMEM((tiles, toks, LANES), F32),
            pltpu.VMEM((tiles, toks, LANES), F32),
            pltpu.VMEM((tiles, toks // 2, LANES), F32),
            pltpu.VMEM((toks // 2, LANES), F32),
            pltpu.VMEM((toks // 2, channels), BF16),
            pltpu.VMEM((toks // 2, channels), BF16),
            pltpu.VMEM((channels, dout), BF16),
            pltpu.VMEM((toks // 2, WIDTH), F32),
            pltpu.VMEM((2, tiles, modes, CHUNKS, LANES), F32),
            pltpu.VMEM((tiles, modes, CHUNKS, LANES), F32),
            pltpu.VMEM((8, channels), F32),
            pltpu.VMEM((8, channels), F32),
            pltpu.VMEM((modes, channels), BF16),
            pltpu.VMEM((modes, channels), BF16),
            pltpu.VMEM((modes, channels), BF16),
            pltpu.VMEM((n_ctx // 2, modes, channels), BF16),
            pltpu.VMEM((modes, channels), F32),
            pltpu.VMEM((modes, channels), F32),
            pltpu.VMEM((modes, channels), F32),
            pltpu.VMEM((modes, channels), F32),
            pltpu.VMEM((n_out, share, WIDTH), F32),
            pltpu.VMEM((n_out, share, WIDTH), F32),
            pltpu.VMEM((n_out, share, WIDTH), BF16),
            pltpu.VMEM((n_out, share, WIDTH), BF16),
            pltpu.VMEM((n_out, share, WIDTH), BF16),
            pltpu.VMEM((n_out, share, WIDTH), BF16),
            pltpu.VMEM((n_out, share, WIDTH), BF16),
            pltpu.VMEM((n_out, share, WIDTH), BF16),
            dma, dma, dma((2,)),
            dma((GROUPS,)), dma((GROUPS,)),
            dma((n_ctx // 2, GROUPS)), dma((n_ctx // 2, GROUPS)),
            dma((n_out,)), dma((n_out,)), dma((n_out,)), dma((n_out,)),
            dma((n_out,)), dma((n_out,)),
        ],
        compiler_params=pltpu.CompilerParams(
            collective_id=0, has_side_effects=True, vmem_limit_bytes=58 * 2**20
        ),
    )(x, short_filter, decay_rates, residues, out_weight)


def solution(mesh):
    placed = (
        P("ctx", None, "tp"),
        P(None, None, "tp"),
        P(None, "tp"),
        P(None, "tp"),
        P("tp", None),
    )
    return jax.shard_map(
        functools.partial(per_device, mesh.shape["ctx"]),
        mesh=mesh, in_specs=placed, out_specs=P(("ctx", "tp"), None), check_vma=False,
    )
```

time: 45.8 us -> 42 us (0.917); the launches traced: 45.1 us -> 41.8 us
  Pallas kernels: 43.2 us -> 40 us
    pallas_call x1, Pallas kernels: 43.2 us -> 40 us  [per_device(): pl.pallas_call(functools.partial(kernel, n_ctx), out_shape=jax.ShapeDtype...]
where the time goes in v2:
time: 42 us; the launch traced here: 41.8 us
  Pallas kernels  40 us (95%)
  local copies, waits for them, and re-layouts  1.87 us (4%)
    pallas_call x1, Pallas kernels, per_device(): pl.pallas_call(functools.partial(kernel, n_ctx), out_shape=jax.ShapeDtype...  40 us
    unnamed x1, local copies, waits for them, and re-layouts  1.87 us

profile of v2, /device:TPU:0, one launch (start us, length us, event | category | flops | bytes accessed | tf_op | source)
XLA Modules:
  0.0 41.8 jit_solution(16309153118812440869)
XLA Ops:
  0.0 40.0 %shard_map.55 = bf16[64,4096]{1,0:T(8,128)(2,1)} custom-call(bf16[3,256,2048]{2,1,0:T(8,128)(2,1)} %bitcast.1, f32[3,3,2048]{2,1,0:T(4,128)} %taps_ref.1, f32[16,2048]{1,0:T(8,128)} %rates_ref.1, f32[16,2048]{1,0:T(8,128)} %res_ref.1, bf16[2048,4096]{1,0:T(8,128)(2,1)} %w_hbm.1), custom_call_target="tpu_custom_call" | custom-call | tf_op jit(solution)/shard_map/pallas_call | solution.py:370
  40.0 1.9 %copy.7 = bf16[64,4096]{1,0:T(8,128)(2,1)} copy(bf16[64,4096]{1,0:T(8,128)(2,1)} %shard_map.55) | data formatting | bytes 1048576

commit v3 on v2

--- a/solution.py
+++ b/solution.py
@@ -42,13 +42,14 @@
     toks, channels = xb.shape[1], xb.shape[2]
     half = toks // 2
     step = half // CHUNKS
+    apart = step + 1
     tiles = channels // LANES
     per_group = tiles // GROUPS
     gwidth = channels // GROUPS
     n_out = w_hbm.shape[1] // WIDTH
     share = toks // 4
-    base_a = pl.multiple_of((1 - chip) * half, half)
-    base_b = pl.multiple_of(chip * half, half)
+    base_a = (1 - chip) * (CHUNKS * apart)
+    base_b = chip * (CHUNKS * apart)
 
     x_copy = pltpu.make_async_copy(x_hbm, xb, x_sem)
     x_copy.start()
@@ -90,8 +91,12 @@
             for i in (1, 2):
                 total += taps_ref[i, j : j + 1, lane] * xs[j, c, PAD - i : PAD - i + rows, :]
             feats.append(total)
-        qf[c, :rows, :] = feats[0]
-        pf[c, :rows, :] = feats[1] * feats[2]
+        product = feats[1] * feats[2]
+        for low in range(0, rows, step):
+            high = min(low + step, rows)
+            at = low // step * apart
+            qf[c, at : at + high - low, :] = feats[0][low:high]
+            pf[c, at : at + high - low, :] = product[low:high]
 
     @pl.loop(0, tiles)
     def _(c):
@@ -133,7 +138,7 @@
 
         def ends(outer, state):
             for k in range(UNROLL):
-                rows = pl.ds(base_b + outer * UNROLL + k, CHUNKS, stride=step)
+                rows = pl.ds(base_b + outer * UNROLL + k, CHUNKS, stride=apart)
                 state = decay * state + pf[c, rows, :][None]
             return state
 
@@ -142,9 +147,9 @@
 
         def both(outer, state):
             for k in range(UNROLL):
-                rows = pl.ds(base_a + outer * UNROLL + k, CHUNKS, stride=step)
+                rows = pl.ds(base_a + outer * UNROLL + k, CHUNKS, stride=apart)
                 state = decay * state + pf[c, rows, :][None]
-                yl[c, pl.ds(outer * UNROLL + k, CHUNKS, stride=step), :] = summed(weight * state)
+                yl[c, pl.ds(outer * UNROLL + k, CHUNKS, stride=apart), :] = summed(weight * state)
             return state
 
         before_a, total_a = scanned(lax.fori_loop(0, step // UNROLL, both, zero), rates)
@@ -230,14 +235,15 @@
         def some(outer, state):
             for k in range(UNROLL):
                 i = outer * UNROLL + k
-                local = pl.ds(i, CHUNKS, stride=step)
-                gate = qf[c, pl.ds(base_a + i, CHUNKS, stride=step), :]
+                local = pl.ds(i, CHUNKS, stride=apart)
+                gate = qf[c, pl.ds(base_a + i, CHUNKS, stride=apart), :]
                 gs[local, :] = gate * (yl[c, local, :] + summed(state))
                 state = decay * state
             return state
 
         lax.fori_loop(0, step // UNROLL, some, state)
-        ga[:, lane] = gs[...].astype(BF16)
+        for s in range(CHUNKS):
+            ga[s * step : (s + 1) * step, lane] = gs[s * apart : s * apart + step, :].astype(BF16)
 
     def own_tile(c):
         lane = pl.ds(pl.multiple_of(c * LANES, LANES), LANES)
@@ -249,13 +255,14 @@
         def some(outer, state):
             for k in range(UNROLL):
                 i = outer * UNROLL + k
-                rows = pl.ds(base_b + i, CHUNKS, stride=step)
+                rows = pl.ds(base_b + i, CHUNKS, stride=apart)
                 state = decay * state + pf[c, rows, :][None]
-                gs[pl.ds(i, CHUNKS, stride=step), :] = qf[c, rows, :] * summed(weight * state)
+                gs[pl.ds(i, CHUNKS, stride=apart), :] = qf[c, rows, :] * summed(weight * state)
             return state
 
         lax.fori_loop(0, step // UNROLL, some, state)
-        gb[:, lane] = gs[...].astype(BF16)
+        for s in range(CHUNKS):
+            gb[s * step : (s + 1) * step, lane] = gs[s * apart : s * apart + step, :].astype(BF16)
 
     for g in range(GROUPS):
         cols = group(g)
@@ -364,6 +371,7 @@
     tiles = channels // LANES
     n_out = dout // WIDTH
     share = toks // 4
+    padded = toks // 2 + CHUNKS
     dma = pltpu.SemaphoreType.DMA
     vmem = pl.BlockSpec(memory_space=pltpu.VMEM)
     hbm = pl.BlockSpec(memory_space=pl.ANY)
@@ -375,10 +383,10 @@
         scratch_shapes=[
             pltpu.VMEM((3, toks, channels), BF16),
             pltpu.VMEM((3, tiles, PAD + toks, LANES), F32),
-            pltpu.VMEM((tiles, toks, LANES), F32),
-            pltpu.VMEM((tiles, toks, LANES), F32),
-            pltpu.VMEM((tiles, toks // 2, LANES), F32),
-            pltpu.VMEM((toks // 2, LANES), F32),
+            pltpu.VMEM((tiles, 2 * padded, LANES), F32),
+            pltpu.VMEM((tiles, 2 * padded, LANES), F32),
+            pltpu.VMEM((tiles, padded, LANES), F32),
+            pltpu.VMEM((padded, LANES), F32),
             pltpu.VMEM((toks // 2, channels), BF16),
             pltpu.VMEM((toks // 2, channels), BF16),
             pltpu.VMEM((channels, dout), BF16),

time: 42 us -> 41.4 us (0.986)
  Pallas kernels: 40 us -> 39.3 us
    pallas_call x1, Pallas kernels: 40 us -> 39.3 us  [per_device(): pl.pallas_call(functools.partial(kernel, n_ctx), out_shape=jax.ShapeDtype...]
where the time goes in v3:
time: 41.4 us; the launch traced here: 41.2 us
  Pallas kernels  39.3 us (95%)
  local copies, waits for them, and re-layouts  1.87 us (5%)
    pallas_call x1, Pallas kernels, per_device(): pl.pallas_call(functools.partial(kernel, n_ctx), out_shape=jax.ShapeDtype...  39.3 us
    unnamed x1, local copies, waits for them, and re-layouts  1.87 us

profile of v3, /device:TPU:0, one launch (start us, length us, event | category | flops | bytes accessed | tf_op | source)
XLA Modules:
  0.0 41.2 jit_solution(15053884316561040986)
XLA Ops:
  0.0 39.3 %shard_map.55 = bf16[64,4096]{1,0:T(8,128)(2,1)} custom-call(bf16[3,256,2048]{2,1,0:T(8,128)(2,1)} %bitcast.1, f32[3,3,2048]{2,1,0:T(4,128)} %taps_ref.1, f32[16,2048]{1,0:T(8,128)} %rates_ref.1, f32[16,2048]{1,0:T(8,128)} %res_ref.1, bf16[2048,4096]{1,0:T(8,128)(2,1)} %w_hbm.1), custom_call_target="tpu_custom_call" | custom-call | tf_op jit(solution)/shard_map/pallas_call | solution.py:378
  39.3 1.9 %copy.7 = bf16[64,4096]{1,0:T(8,128)(2,1)} copy(bf16[64,4096]{1,0:T(8,128)(2,1)} %shard_map.55) | data formatting | bytes 1048576
